TPU v7x, 32 devices: a whole 2x2x4 slice. The times are simulated.
32 devices in a mesh: ga: 2 (over y), gx: 4 (over z), yz: 4 (over x, core).
Axes of the slice: x: 2, y: 2, z: 4, core: 2. Of those that a mesh axis runs over, the one named last changes fastest.
Arguments:
- tokens: bfloat16 [128, 18432], P(('ga', 'yz'), 'gx'), parts along dimension 0, may hold values from -6 to 6
- w_query: bfloat16 [18432, 12288], P('gx', 'yz'), may hold values from -0.046875 to 0.046875
- w_keyval: bfloat16 [18432, 512], P('gx', 'yz'), may hold values from -0.046875 to 0.046875
- w_out: bfloat16 [12288, 18432], P('yz', 'gx'), may hold values from -0.4375 to 0.4375
- cache_keys: bfloat16 [128, 512, 256], P(('ga', 'yz'), 'gx'), parts along dimension 0, may hold values from -720 to 720
- cache_values: bfloat16 [128, 512, 256], P(('ga', 'yz'), 'gx'), parts along dimension 0, may hold values from -6 to 6
- lengths: int32 [128], P(('ga', 'yz')), parts along dimension 0, may hold values from 128 to 512, as said below
- positions: int32 [128], P(('ga', 'yz')), parts along dimension 0, may hold values from 0 to 4095
Outputs:
- attended: bfloat16 [128, 18432], P(('ga', 'yz'), 'gx'), parts along dimension 0
There are 2 independent parts, one for each index of `ga`. A program takes and returns all parts, laid end to end along the dimension named above; an argument that names none is the same for every part. Nothing has to cross between parts.
Inputs may be any that keep to these rules, and one draw needn't show every extreme that they name: `lengths`: some row holds all 512 slots and some row a quarter of them.
All inputs are finite; a program needn't handle non-finite values.
Results may differ from a plain program's by a relative error of at most 0.0055.
The roundings to bfloat16 on the way count: a program that leaves them out, or rounds other values in their place, can miss the bound.
Values may be sent and summed in bfloat16 or wider, within the bound.
A program may use at most 128 MiB of HBM per device.

v0:
```python
import math

import jax
import jax.numpy as jnp
from jax import lax
from jax.sharding import PartitionSpec as P

HEAD_DIM = 256


def merged(array, axis, combine):
    everything = jax.tree.map(lambda part: lax.all_gather(part, axis), array)
    leading = jax.tree.map(lambda part: part[0], everything)

    def hop(k, so_far):
        return combine(so_far, jax.tree.map(lambda part: part[k], everything))

    return lax.fori_loop(1, lax.axis_size(axis), hop, leading)


def rotate(vectors, angles):
    half_dim = vectors.shape[-1] // 2
    first_half = vectors[..., :half_dim]
    second_half = vectors[..., half_dim:]
    cosines = jnp.cos(angles)
    sines = jnp.sin(angles)
    return jnp.concatenate(
        [first_half * cosines - second_half * sines, first_half * sines + second_half * cosines],
        axis=-1,
    )


def rotary_angles(positions, head_dim):
    half_dim = head_dim // 2
    inv_freq = jnp.exp(-jnp.arange(half_dim, dtype=jnp.float32) * (math.log(10000.0) / half_dim))
    return positions.astype(jnp.float32)[:, None] * inv_freq[None, :]


def combine(former, latter):
    peak_a, mass_a, summed_a = former
    peak_b, mass_b, summed_b = latter
    highest = jnp.maximum(peak_a, peak_b)
    factor_a = jnp.exp(peak_a - highest)
    factor_b = jnp.exp(peak_b - highest)
    return (
        highest,
        mass_a * factor_a + mass_b * factor_b,
        summed_a * factor_a[..., None] + summed_b * factor_b[..., None],
    )


def body(tokens, w_query, w_keyval, w_out, cache_keys, cache_values, lengths, positions):
    query_cols = w_query.shape[1]
    block_rows = lax.all_gather(tokens, "yz", axis=0, tiled=True)
    partial_proj = jnp.concatenate(
        [
            jnp.dot(block_rows, w_query, preferred_element_type=jnp.float32),
            jnp.dot(block_rows, w_keyval, preferred_element_type=jnp.float32),
        ],
        axis=1,
    )
    query_part = partial_proj[:, :query_cols]
    keyval_part = partial_proj[:, query_cols:]
    query_sum, keyval_sum = lax.psum((query_part, keyval_part), "gx")
    query_full = query_sum.astype(jnp.bfloat16)
    keyval_full = keyval_sum.astype(jnp.bfloat16)
    query_rows, keyval_rows = (
        lax.all_to_all(query_full, "yz", split_axis=0, concat_axis=1, tiled=True),
        lax.all_to_all(keyval_full, "yz", split_axis=0, concat_axis=1, tiled=True),
    )
    row_count = query_rows.shape[0]
    head_count = query_rows.shape[1] // HEAD_DIM
    angles = rotary_angles(positions, HEAD_DIM)
    rot_query = rotate(
        query_rows.astype(jnp.float32).reshape(row_count, head_count, HEAD_DIM), angles[:, None, :]
    )
    rot_key = rotate(keyval_rows[:, :HEAD_DIM].astype(jnp.float32), angles)
    new_value = keyval_rows[:, HEAD_DIM:].astype(jnp.float32)
    score_scale = HEAD_DIM ** (-0.5)
    local_span = cache_keys.shape[1]
    slots_at = lax.axis_index("gx") * local_span + jnp.arange(local_span, dtype=jnp.int32)
    visible = slots_at[None, :] < lengths[:, None]
    scores = (
        jnp.einsum(
            "rhd,rtd->rht",
            rot_query,
            cache_keys.astype(jnp.float32),
            precision=lax.Precision.HIGHEST,
        )
        * score_scale
    )
    scores = jnp.where(visible[:, None, :], scores, jnp.float32(-1e30))
    row_peak = jnp.max(scores, axis=2)
    weights = jnp.where(
        visible[:, None, :], jnp.exp(scores - row_peak[..., None]), jnp.float32(0.0)
    )
    row_mass = jnp.sum(weights, axis=2)
    weighted = jnp.einsum(
        "rht,rtd->rhd", weights, cache_values.astype(jnp.float32), precision=lax.Precision.HIGHEST
    )
    row_peak, row_mass, weighted = merged((row_peak, row_mass, weighted), "gx", combine)
    new_score = (
        jnp.einsum("rhd,rd->rh", rot_query, rot_key, precision=lax.Precision.HIGHEST) * score_scale
    )
    highest = jnp.maximum(row_peak, new_score)
    old_factor = jnp.exp(row_peak - highest)
    new_weight = jnp.exp(new_score - highest)
    normaliser = row_mass * old_factor + new_weight
    summed = weighted * old_factor[..., None] + new_weight[..., None] * new_value[:, None, :]
    out_heads = (
        (summed / normaliser[..., None])
        .reshape(row_count, head_count * HEAD_DIM)
        .astype(jnp.bfloat16)
    )
    heads_local = lax.all_to_all(out_heads, "yz", split_axis=1, concat_axis=0, tiled=True)
    block_rows = heads_local
    attended = lax.psum_scatter(
        jnp.dot(block_rows, w_out, preferred_element_type=jnp.float32),
        "yz",
        scatter_dimension=0,
        tiled=True,
    )
    return attended.astype(jnp.bfloat16)


def solution(mesh):
    placed = (
        P(("ga", "yz"), "gx"),
        P("gx", "yz"),
        P("gx", "yz"),
        P("yz", "gx"),
        P(("ga", "yz"), "gx", None),
        P(("ga", "yz"), "gx", None),
        P(("ga", "yz")),
        P(("ga", "yz")),
    )
    return jax.shard_map(
        body, mesh=mesh, in_specs=placed, out_specs=P(("ga", "yz"), "gx"), check_vma=False
    )
```

profile of v0, /device:TPU:0, one launch (start us, length us, event | category | flops | bytes accessed | tf_op | source)
XLA Modules:
  0.0 211.8 jit_solution(8669765090458663595)
XLA Ops:
  6.5 9.3 %all_gather.21 = bf16[64,4608]{1,0:T(8,128)(2,1)S(1)} all-gather(bf16[16,4608]{1,0:T(8,128)(2,1)} %param.10), channel_id=1, replica_groups=mesh['ga'=2,'gx'=4,'yz'=4] {'yz'}, dimensions={0}, use_global_device_ids=true | all-gather | bytes 737280 | tf_op jit(solution)/shard_map/all_gather | solution.py:54
  15.9 0.4 fusion.21
  16.2 11.6 %fusion.20 = f32[64,3072]{1,0:T(8,128)S(1)} fusion(bf16[64,4608]{1,0:T(8,128)(2,1)S(1)} %all_gather.21, bf16[4608,3072]{1,0:T(8,128)(2,1)} %param.11), kind=kOutput, calls=%fused_computation.43 | convolution fusion | flops 1811939328 | bytes 29687808 | tf_op jit(solution)/shard_map/dot_general | solution.py:57
  27.9 37.8 %all-reduce.2 = (bf16[64,3072]{1,0:T(8,128)(2,1)}, bf16[64,128]{1,0:T(8,128)(2,1)}) all-reduce(f32[64,3072]{1,0:T(8,128)S(1)} %fusion.20, f32[64,128]{1,0:T(8,128)S(1)} %fusion.21), channel_id=1, replica_groups=mesh['ga'=2,'gx'=4,'yz'=4] {'gx'}, use_global_device_ids=true, to_apply=%region_0.0 | all-reduce | flops 204800 | bytes 1228800 | tf_op jit(solution)/shard_map/psum | solution.py:64
  65.6 3.3 %all-to-all-start.1 = ((bf16[4,16,128]{2,1,0:T(8,128)(2,1)}), bf16[4,16,128]{2,1,0:T(8,128)(2,1)S(1)}, u32[]{:S(2)}, u32[]{:S(2)}) async-start(bf16[4,16,128]{2,1,0:T(8,128)(2,1)} %bitcast.8), calls=%async_computation.1 | async-start | bytes 32768 | tf_op jit(solution)/shard_map/all_to_all | solution.py:69
  68.9 0.1 broadcast_compare_fusion
  69.0 3.7 %all-to-all-done.1 = bf16[4,16,128]{2,1,0:T(8,128)(2,1)S(1)} async-done(((bf16[4,16,128]{2,1,0:T(8,128)(2,1)}), bf16[4,16,128]{2,1,0:T(8,128)(2,1)S(1)}, u32[]{:S(2)}, u32[]{:S(2)}) %all-to-all-start.1) | async-done | bytes 16416 | tf_op jit(solution)/shard_map/all_to_all | solution.py:69
  72.7 3.5 %all-to-all-start = ((bf16[4,16,3072]{2,1,0:T(8,128)(2,1)}), bf16[4,16,3072]{2,1,0:T(8,128)(2,1)S(1)}, u32[]{:S(2)}, u32[]{:S(2)}) async-start(bf16[4,16,3072]{2,1,0:T(8,128)(2,1)} %bitcast.3), calls=%async_computation | async-start | bytes 786432 | tf_op jit(solution)/shard_map/all_to_all | solution.py:68
  76.3 0.1 multiply_subtract_fusion.1
  76.4 7.2 %all-to-all-done = bf16[4,16,3072]{2,1,0:T(8,128)(2,1)S(1)} async-done(((bf16[4,16,3072]{2,1,0:T(8,128)(2,1)}), bf16[4,16,3072]{2,1,0:T(8,128)(2,1)S(1)}, u32[]{:S(2)}, u32[]{:S(2)}) %all-to-all-start) | async-done | bytes 393248 | tf_op jit(solution)/shard_map/all_to_all | solution.py:68
  83.6 0.5 copy.16
  84.2 0.4 reshape.103
  84.6 0.1 multiply_subtract_fusion
  84.7 1.3 fusion.19
  86.0 2.8 %fusion.5 = f32[16,48,256]{2,1,0:T(8,128)} fusion(bf16[16,128,256]{2,1,0:T(8,128)(2,1)} %param.15, f32[16,48,128]{2,1,0:T(8,128)S(1)} %get-tuple-element.218, f32[16,48]{1,0:T(8,128)S(1)} %get-tuple-element.217, pred[16,128]{1,0:T(8,128)(4,1)S(1)} %broadcast_compare_fusion), kind=kOutput, calls=%fused_computation.17 | convolution fusion | flops 302186496 | bytes 2233344 | tf_op jit(solution)/shard_map/rht,rtd->rhd/dot_general | solution.py:98
  88.9 0.3 fusion.6
  89.2 13.3 %all-gather.1 = f32[64,48]{1,0:T(8,128)S(1)} all-gather(f32[16,48]{1,0:T(8,128)S(1)} %fusion.6), channel_id=3, replica_groups=mesh['ga'=2,'gx'=4,'yz'=4] {'gx'}, dimensions={0}, use_global_device_ids=true | all-gather | bytes 15360 | tf_op jit(solution)/shard_map/all_gather | solution.py:12
  102.5 13.4 %all-gather = f32[64,48]{1,0:T(8,128)S(1)} all-gather(f32[16,48]{1,0:T(8,128)S(1)} %get-tuple-element.217), channel_id=2, replica_groups=mesh['ga'=2,'gx'=4,'yz'=4] {'gx'}, dimensions={0}, use_global_device_ids=true | all-gather | bytes 15360 | tf_op jit(solution)/shard_map/all_gather | solution.py:12
  115.8 0.8 fusion.4
  116.6 34.0 %all-gather.5.cloned.1.call-done = f32[64,48,256]{2,1,0:T(8,128)} async-done(((f32[16,48,256]{2,1,0:T(8,128)}), f32[64,48,256]{2,1,0:T(8,128)}) %all-gather.5.cloned.1.call-update) | async-done | bytes 3145744 | tf_op jit(solution)/shard_map/all_gather | solution.py:12
  150.6 1.2 slice.43
  151.8 4.6 %while.19 = (s32[]{:T(128)}, f32[16,48]{1,0:T(8,128)S(1)}, f32[16,48]{1,0:T(8,128)S(1)}, f32[16,48,256]{2,1,0:T(8,128)S(1)}, f32[4,16,48]{2,1,0:T(8,128)S(1)}, /...) while((s32[]{:T(128)}, f32[16,48]{1,0:T(8,128)S(1)}, ...), condition=%wide.region_4.5_spmd, body=%wide.region_3.4_spmd.sunk | while | flops 594437 | bytes 2390159 | solution.py:18
  151.9 1.5 fusion.35
  153.4 1.5 fusion.35
  154.9 1.5 fusion.35
  156.5 0.4 divide_convert_fusion
  156.9 0.1 convert_element_type.46
  157.0 0.1 copy.18
  157.1 9.9 %all_to_all.48 = bf16[16,4,3072]{2,0,1:T(8,128)(2,1)S(1)} all-to-all(bf16[16,4,3072]{2,0,1:T(8,128)(2,1)S(1)} %copy.18), channel_id=1, replica_groups=mesh['ga'=2,'gx'=4,'yz'=4] {'yz'}, dimensions={1} | all-to-all | bytes 786432 | tf_op jit(solution)/shard_map/all_to_all | solution.py:115
  167.0 12.6 %fusion.22 = f32[64,4608]{1,0:T(8,128)} fusion(bf16[64,3072]{1,0:T(8,128)(2,1)S(1)} %bitcast.48, bf16[3072,4608]{1,0:T(8,128)(2,1)} %param.13), kind=kOutput, calls=%fused_computation.45 | convolution fusion | flops 1811939328 | bytes 29884416 | tf_op jit(solution)/shard_map/dot_general | solution.py:118
  179.7 23.7 %reduce-scatter.2.cloned.1.call-done = f32[16,4608]{1,0:T(8,128)} async-done(((f32[64,4608]{1,0:T(8,128)}), f32[16,4608]{1,0:T(8,128)}) %reduce-scatter.2.cloned.1.call-update) | async-done | bytes 294928 | tf_op jit(solution)/shard_map/reduce_scatter | solution.py:117
  203.4 1.6 convert_element_type.47
  (27 shorter events, 0.3 us)
Async XLA Ops:
  6.5 9.3 %copy-start = (bf16[4608,128]{1,0:T(8,128)(2,1)S(1)}, bf16[4608,128]{1,0:T(8,128)(2,1)}, u32[]{:S(2)}) copy-start(bf16[4608,128]{1,0:T(8,128)(2,1)} %param.12) | copy-start | bytes 3538948
  6.5 62.4 %copy-start.3 = (s32[16]{0:T(128)S(1)}, s32[16]{0:T(128)}, u32[]{:S(2)}) copy-start(s32[16]{0:T(128)} %param.16) | copy-start | bytes 196
  6.5 62.5 %copy-start.4 = (s32[16]{0:T(128)S(1)}, s32[16]{0:T(128)}, u32[]{:S(2)}) copy-start(s32[16]{0:T(128)} %param.17) | copy-start | bytes 196
  6.5 78.1 %copy-start.2 = (bf16[16,128,256]{2,1,0:T(8,128)(2,1)S(1)}, bf16[16,128,256]{2,1,0:T(8,128)(2,1)}, u32[]{:S(2)}) copy-start(bf16[16,128,256]{2,1,0:T(8,128)(2,1)} %param.14) | copy-start | bytes 3145732
  65.6 7.1 %all-to-all-start.1 = ((bf16[4,16,128]{2,1,0:T(8,128)(2,1)}), bf16[4,16,128]{2,1,0:T(8,128)(2,1)S(1)}, u32[]{:S(2)}, u32[]{:S(2)}) async-start(bf16[4,16,128]{2,1,0:T(8,128)(2,1)} %bitcast.8), calls=%async_computation.1 | async-start | bytes 32768 | tf_op jit(solution)/shard_map/all_to_all | solution.py:69
  72.7 10.9 %all-to-all-start = ((bf16[4,16,3072]{2,1,0:T(8,128)(2,1)}), bf16[4,16,3072]{2,1,0:T(8,128)(2,1)S(1)}, u32[]{:S(2)}, u32[]{:S(2)}) async-start(bf16[4,16,3072]{2,1,0:T(8,128)(2,1)} %bitcast.3), calls=%async_computation | async-start | bytes 786432 | tf_op jit(solution)/shard_map/all_to_all | solution.py:68
  76.2 74.5 %all-gather.5.cloned.1.call-start = ((), (), s32[]{:S(2)}) async-start(), calls=%async_computation.5 | async-start | bytes 3932160 | tf_op jit(solution)/shard_map/all_gather | solution.py:12
  85.9 119.1 %copy-start.1 = (bf16[4608,128]{1,0:T(8,128)(2,1)S(1)}, bf16[4608,128]{1,0:T(8,128)(2,1)}, u32[]{:S(2)}) copy-start(bf16[4608,128]{1,0:T(8,128)(2,1)} %param.12) | copy-start | bytes 3538948
  88.8 114.5 %reduce-scatter.2.cloned.1.call-start = ((), (), s32[]{:S(2)}) async-start(), calls=%async_computation.4 | async-start | bytes 1474560 | tf_op jit(solution)/shard_map/reduce_scatter | solution.py:117
Sparse Core Ops, SparseCore 0:
  88.9 61.6 all-gather.4
  179.8 23.5 reduce-scatter.1
where the time goes:
time: 212 us
  blocking collectives  83.6 us (39%)
  waiting for transfers between devices  68.6 us (32%)
  matrix products  29.5 us (14%)
  between operations  13.6 us (6%)
  other arithmetic  7.26 us (3%)
  starting transfers between devices  6.8 us (3%)
  local copies, waits for them, and re-layouts  2.4 us (1%)
    psum x1, blocking collectives, body(): query_sum, keyval_sum = lax.psum((query_part, keyval_part), 'gx')  37.8 us
    all_gather x1, waiting for transfers between devices, merged(): everything = jax.tree.map(lambda part: lax.all_gather(part, axis), array)  34 us
    all_gather x2, blocking collectives, merged(): everything = jax.tree.map(lambda part: lax.all_gather(part, axis), array)  26.6 us
    reduce_scatter x1, waiting for transfers between devices, body(): lax.psum_scatter(jnp.dot(block_rows, w_out, preferred_element_type=jnp.fl...  23.7 us
    dot_general x1, matrix products, body(): jnp.dot(block_rows, w_out, preferred_element_type=jnp.float32)  12.6 us
    dot_general x1, matrix products, body(): jnp.dot(block_rows, w_query, preferred_element_type=jnp.float32)  11.6 us
    all_to_all x1, blocking collectives, body(): lax.all_to_all(out_heads, 'yz', split_axis=1, concat_axis=0, tiled=True)  9.89 us
    all_gather x1, blocking collectives, body(): block_rows = lax.all_gather(tokens, 'yz', axis=0, tiled=True)  9.31 us
  transfers between devices with their start and end apart: 4, of which 4 were waited for; matrix products, arithmetic and copies ran while one was open for 1% of the time, Pallas kernels for 0%

commit v1 on v0

--- a/solution.py
+++ b/solution.py
@@ -1,11 +1,16 @@
+import functools
 import math
 
 import jax
 import jax.numpy as jnp
 from jax import lax
+from jax.experimental import pallas as pl
+from jax.experimental.pallas import tpu as pltpu
 from jax.sharding import PartitionSpec as P
 
 HEAD_DIM = 256
+MESH = pl.DeviceIdType.MESH
+VMEM_LIMIT = 64 * 1024 * 1024 - 65536
 
 
 def merged(array, axis, combine):
@@ -123,6 +128,412 @@
     return attended.astype(jnp.bfloat16)
 
 
+def fits(mesh, w_query):
+    z_count, y_count = mesh.shape["gx"], mesh.shape["yz"]
+    heads_local = w_query.shape[1] // HEAD_DIM // y_count
+    return heads_local % z_count == 0 and z_count > 1 and y_count > 1 and (w_query.shape[0] // z_count) % 512 == 0
+
+
+def split3(x):
+    first = x.astype(jnp.bfloat16)
+    rest = x - first.astype(jnp.float32)
+    second = rest.astype(jnp.bfloat16)
+    third = (rest - second.astype(jnp.float32)).astype(jnp.bfloat16)
+    return first, second, third
+
+
+def fused_kernel(
+    dims,
+    len_ref, tok_ref, cos_ref, sin_ref, wq_ref, wkv_ref, wo_ref, ck_ref, cv_ref,
+    out_ref,
+    wq, wkv, wo, kc, vc, tok, part, rbuf, kvp, kvr, kvs, kvin, qs, qin, ra, rb, rk,
+    s_buf, sn_buf, st, str_, mg, lg, oa, ob, oar, obr, hs, xin, pout, prc,
+    wq_sem, misc_sem, wo_sem, tok_s, tok_r, rs_s, rs_r, kv_s, kv_r, kv2_s, kv2_r,
+    qd_s, qd_r, st_s, st_r, oa_s, oa_r, ob_s, ob_r, hd_s, hd_r, po_s, po_r,
+):
+    NZ, NY, R, HL, SLOTS, CH, NCH = dims
+    HEADS = HL * NY
+    HZ = HL // NZ
+    W = HZ * HEAD_DIM
+    z = lax.axis_index("gx")
+    y = lax.axis_index("yz")
+    f32 = jnp.float32
+
+    def peer(dz, dy):
+        return {"gx": lax.rem(z + dz, NZ), "yz": lax.rem(y + dy, NY)}
+
+    def remote(src, dst, s, r, dev):
+        return pltpu.make_async_remote_copy(
+            src_ref=src, dst_ref=dst, send_sem=s, recv_sem=r, device_id=dev, device_id_type=MESH
+        )
+
+    SLOTSQ = wq.shape[0]
+
+    def wq_copy(n):
+        owner = lax.rem(z + n // HZ + 1, NZ)
+        col = pl.multiple_of((owner * HZ + n % HZ) * HEAD_DIM, HEAD_DIM)
+        slot = lax.rem(n, SLOTSQ)
+        return pltpu.make_async_copy(wq_ref.at[:, pl.ds(col, HEAD_DIM)], wq.at[slot], wq_sem.at[slot])
+
+    own_rows = pl.ds(pl.multiple_of(y * R, R), R)
+    tok_local = pltpu.make_async_copy(tok_ref, tok.at[own_rows, :], misc_sem.at[0])
+    tok_local.start()
+    wkv_local = pltpu.make_async_copy(wkv_ref, wkv, misc_sem.at[1])
+    kc_local = pltpu.make_async_copy(ck_ref, kc, misc_sem.at[2])
+    vc_local = pltpu.make_async_copy(cv_ref, vc.at[:, pl.ds(0, SLOTS), :], misc_sem.at[3])
+
+    barrier = pltpu.get_barrier_semaphore()
+
+    @pl.loop(1, NZ * NY)
+    def _(o):
+        pl.semaphore_signal(barrier, inc=1, device_id=peer(o // NY, o % NY), device_id_type=MESH)
+
+    pl.semaphore_wait(barrier, NZ * NY - 1)
+
+    def tok_copy(d):
+        return remote(tok_ref, tok.at[own_rows, :], tok_s.at[d - 1], tok_r.at[d - 1], peer(0, d))
+
+    for d in range(1, NY):
+        tok_copy(d).start()
+    wkv_local.start()
+
+    @pl.loop(0, SLOTSQ)
+    def _(n):
+        wq_copy(n).start()
+
+    kc_local.start()
+    vc_local.start()
+
+    def wo_copy(n):
+        col = pl.multiple_of(n * CH, CH)
+        return pltpu.make_async_copy(wo_ref.at[:, pl.ds(col, CH)], wo.at[n], wo_sem.at[n])
+
+    tok_local.wait()
+    for d in range(1, NY):
+        tok_copy(d).wait_recv()
+
+    wkv_local.wait()
+    kvp[...] = jnp.dot(tok[...], wkv[...], preferred_element_type=f32)
+
+    def kv_copy(slot):
+        return remote(kvp, kvr.at[slot], kv_s, kv_r.at[slot], {"gx": 0, "yz": y})
+
+    for src in range(1, NZ):
+        @pl.when(z == src)
+        def _():
+            kv_copy(src - 1).start()
+
+    def rs_copy(n):
+        return remote(part.at[n], rbuf.at[n], rs_s.at[n], rs_r.at[n], peer(n // HZ + 1, 0))
+
+    def project(n):
+        wq_copy(n).wait()
+        part[n] = jnp.dot(tok[...], wq[lax.rem(n, SLOTSQ)], preferred_element_type=f32)
+
+        @pl.when(n + SLOTSQ < HL)
+        def _():
+            wq_copy(n + SLOTSQ).start()
+
+    REM = HL - HZ
+
+    @pl.loop(0, REM)
+    def _(n):
+        project(n)
+        rs_copy(n).start()
+
+    @pl.loop(REM, HL)
+    def _(n):
+        project(n)
+
+    @pl.loop(0, NCH)
+    def _(n):
+        wo_copy(n).start()
+
+    def kv2_copy(d):
+        target = lax.rem(y + d, NY)
+        rows = pl.ds(pl.multiple_of(target * R, R), R)
+        return remote(kvs.at[rows, :], kvin.at[y], kv2_s.at[d - 1], kv2_r.at[d - 1], {"gx": 0, "yz": target})
+
+    @pl.when(z == 0)
+    def _():
+        total = kvp[...]
+        for src in range(1, NZ):
+            kv_copy(src - 1).wait_recv()
+            total = total + kvr[src - 1]
+        kvs[...] = total.astype(jnp.bfloat16)
+        for d in range(1, NY):
+            kv2_copy(d).start()
+        kvin[y] = kvs[own_rows, :]
+
+    @pl.when(z != 0)
+    def _():
+        kvin[...] = jnp.zeros_like(kvin)
+
+    for i in range(HZ):
+        total = part[REM + i]
+        for d in range(1, NZ):
+            n = (d - 1) * HZ + i
+            rs_copy(n).wait_recv()
+            total = total + rbuf[n]
+        qs[:, i * HEAD_DIM:(i + 1) * HEAD_DIM] = total.astype(jnp.bfloat16)
+
+    own_cols = pl.ds(pl.multiple_of((y * NZ + z) * W, W), W)
+
+    def qd_copy(o):
+        target = lax.rem(y + o % NY, NY)
+        rows = pl.ds(pl.multiple_of(target * R, R), R)
+        return remote(qs.at[rows, :], qin.at[:, own_cols], qd_s.at[o - 1], qd_r.at[o - 1], peer(o // NY, o % NY))
+
+    @pl.loop(1, NZ * NY)
+    def _(o):
+        qd_copy(o).start()
+
+    qin[:, own_cols] = qs[own_rows, :]
+    kc_local.wait()
+    vc_local.wait()
+
+    cosines = cos_ref[...]
+    sines = sin_ref[...]
+    half = HEAD_DIM // 2
+
+    @pl.when(z == 0)
+    def _():
+        for d in range(1, NY):
+            kv2_copy(d).wait_recv()
+
+    quarter = kvin.shape[2]
+    kv_all = jnp.concatenate([kvin[k].astype(f32) for k in range(NY)], axis=1)
+    ka = kv_all[:, :half]
+    kb = kv_all[:, half:HEAD_DIM]
+    rk[:, :half] = ka * cosines - kb * sines
+    rk[:, half:HEAD_DIM] = ka * sines + kb * cosines
+    rk[:, HEAD_DIM:] = kv_all[:, HEAD_DIM:]
+    st[...] = jnp.zeros_like(st)
+
+    @pl.loop(1, NZ * NY)
+    def _(o):
+        qd_copy(o).wait_recv()
+
+    @pl.loop(0, HEADS)
+    def _(p):
+        owner = p // HL
+        head = (p % HL) // HZ * HL + owner * HZ + p % HZ
+        cols = pl.ds(pl.multiple_of(head * HEAD_DIM, HEAD_DIM), HEAD_DIM)
+        x = qin[:, cols].astype(f32)
+        a = x[:, :half]
+        b = x[:, half:]
+        rows = pl.ds(pl.multiple_of(p * R, R), R)
+        ra[rows, :] = a * cosines - b * sines
+        rb[rows, :] = a * sines + b * cosines
+
+    scale = HEAD_DIM ** (-0.5)
+    over_last = (((1,), (1,)), ((), ()))
+    over_first = (((0,), (0,)), ((), ()))
+    first_z = z == 0
+
+    @pl.loop(0, R)
+    def _(r):
+        picked = pl.ds(r, HEADS, stride=R)
+        q = jnp.concatenate([ra[picked, :], rb[picked, :]], axis=1)
+        keys = kc[r]
+        s = sum(lax.dot_general(keys, piece, over_last, preferred_element_type=f32) for piece in split3(q)) * scale
+        slot = z * SLOTS + lax.broadcasted_iota(jnp.int32, (SLOTS, HEADS), 0)
+        visible = slot < len_ref[r]
+        s = jnp.where(visible, s, f32(-1e30))
+        key_row = jnp.broadcast_to(rk[pl.ds(r, 1), :HEAD_DIM], (8, HEAD_DIM))
+        s_new = lax.dot_general(
+            key_row, q, over_last, precision=lax.Precision.HIGHEST, preferred_element_type=f32
+        )[0:1, :] * scale
+        s_new = jnp.where(first_z, s_new, f32(-1e30))
+        peak = jnp.maximum(jnp.max(s, axis=0, keepdims=True), s_new)
+        mass = jnp.sum(jnp.where(visible, jnp.exp(s - peak), f32(0.0)), axis=0, keepdims=True)
+        mass = mass + jnp.where(first_z, jnp.exp(s_new - peak), f32(0.0))
+        s_buf[r] = s
+        sn_buf[pl.ds(r, 1), :] = s_new
+        st[0, pl.ds(r, 1), 0:HEADS] = peak
+        st[1, pl.ds(r, 1), 0:HEADS] = mass
+        row = lax.broadcasted_iota(jnp.int32, (16, HEAD_DIM), 0)
+        value = jnp.broadcast_to(rk[pl.ds(r, 1), HEAD_DIM:], (16, HEAD_DIM))
+        vc[r, SLOTS:SLOTS + 16, :] = jnp.where(row == 0, value, f32(0.0)).astype(jnp.bfloat16)
+
+    def st_copy(d):
+        return remote(st, str_.at[d - 1], st_s.at[d - 1], st_r.at[d - 1], peer(d, 0))
+
+    for d in range(1, NZ):
+        st_copy(d).start()
+    for d in range(1, NZ):
+        st_copy(d).wait_recv()
+    peak = st[0]
+    for d in range(1, NZ):
+        peak = jnp.maximum(peak, str_[d - 1, 0])
+    mass = st[1] * jnp.exp(st[0] - peak)
+    for d in range(1, NZ):
+        mass = mass + str_[d - 1, 1] * jnp.exp(str_[d - 1, 0] - peak)
+    mg[...] = peak
+    lg[...] = mass
+
+    @pl.loop(0, R)
+    def _(r):
+        peak = mg[pl.ds(r, 1), 0:HEADS]
+        mass = lg[pl.ds(r, 1), 0:HEADS]
+        p = jnp.exp(s_buf[r] - peak) / mass
+        p_new = jnp.exp(sn_buf[pl.ds(r, 1), :] - peak) / mass
+        row = lax.broadcasted_iota(jnp.int32, (16, HEADS), 0)
+        p_new = jnp.where(row == 0, jnp.broadcast_to(p_new, (16, HEADS)), f32(0.0))
+        p_all = jnp.concatenate([p, p_new], axis=0)
+        values = vc[r]
+        acc = sum(lax.dot_general(piece, values, over_first, preferred_element_type=f32) for piece in split3(p_all))
+        picked = pl.ds(r, HEADS, stride=R)
+        oa[picked, :] = acc[:, :half]
+        ob[picked, :] = acc[:, half:]
+
+    def o_copies(d):
+        target = lax.rem(z + d, NZ)
+        rows = pl.ds(pl.multiple_of(target * HL * R, HL * R), HL * R)
+        return (
+            remote(oa.at[rows, :], oar.at[d - 1], oa_s.at[d - 1], oa_r.at[d - 1], peer(d, 0)),
+            remote(ob.at[rows, :], obr.at[d - 1], ob_s.at[d - 1], ob_r.at[d - 1], peer(d, 0)),
+        )
+
+    for d in range(1, NZ):
+        for copy in o_copies(d):
+            copy.start()
+    for d in range(1, NZ):
+        for copy in o_copies(d):
+            copy.wait_recv()
+    for k in range(HL):
+        rows = pl.ds(pl.multiple_of(z * HL * R + k * R, R), R)
+        ta = oa[rows, :]
+        tb = ob[rows, :]
+        for d in range(1, NZ):
+            ta = ta + oar[d - 1, k * R:(k + 1) * R, :]
+            tb = tb + obr[d - 1, k * R:(k + 1) * R, :]
+        block, i = k // HZ, k % HZ
+        hs[block * R:(block + 1) * R, i * HEAD_DIM:i * HEAD_DIM + half] = ta.astype(jnp.bfloat16)
+        hs[block * R:(block + 1) * R, i * HEAD_DIM + half:(i + 1) * HEAD_DIM] = tb.astype(jnp.bfloat16)
+
+    z_cols = pl.ds(pl.multiple_of(z * W, W), W)
+
+    def hd_copy(o):
+        target = lax.rem(y + o % NY, NY)
+        rows = pl.ds(pl.multiple_of(target * R, R), R)
+        return remote(hs.at[rows, :], xin.at[own_rows, z_cols], hd_s.at[o - 1], hd_r.at[o - 1], peer(o // NY, o % NY))
+
+    @pl.loop(1, NZ * NY)
+    def _(o):
+        hd_copy(o).start()
+
+    xin[own_rows, z_cols] = hs[own_rows, :]
+
+    @pl.loop(1, NZ * NY)
+    def _(o):
+        hd_copy(o).wait_recv()
+
+    def po_copy(n, d):
+        target = lax.rem(y + d, NY)
+        rows = pl.ds(pl.multiple_of(target * R, R), R)
+        return remote(
+            pout.at[n, rows, :], prc.at[d - 1, n], po_s.at[d - 1, n], po_r.at[d - 1, n], peer(0, d)
+        )
+
+    @pl.loop(0, NCH)
+    def _(n):
+        wo_copy(n).wait()
+        pout[n] = jnp.dot(xin[...], wo[n], preferred_element_type=f32)
+        for d in range(1, NY):
+            po_copy(n, d).start()
+
+    @pl.loop(0, NCH)
+    def _(n):
+        total = pout[n, own_rows, :]
+        for d in range(1, NY):
+            po_copy(n, d).wait_recv()
+            total = total + prc[d - 1, n]
+        out_ref[:, pl.ds(pl.multiple_of(n * CH, CH), CH)] = total.astype(jnp.bfloat16)
+
+    for d in range(1, NY):
+        tok_copy(d).wait_send()
+    for src in range(1, NZ):
+        @pl.when(z == src)
+        def _():
+            kv_copy(src - 1).wait_send()
+
+    @pl.when(z == 0)
+    def _():
+        for d in range(1, NY):
+            kv2_copy(d).wait_send()
+
+    @pl.loop(0, REM)
+    def _(n):
+        rs_copy(n).wait_send()
+
+    @pl.loop(1, NZ * NY)
+    def _(o):
+        qd_copy(o).wait_send()
+        hd_copy(o).wait_send()
+
+    for d in range(1, NZ):
+        st_copy(d).wait_send()
+        for copy in o_copies(d):
+            copy.wait_send()
+
+    @pl.loop(0, NCH)
+    def _(n):
+        for d in range(1, NY):
+            po_copy(n, d).wait_send()
+
+
+def fused_body(NZ, NY, tokens, w_query, w_keyval, w_out, cache_keys, cache_values, lengths, positions):
+    R, DZ = tokens.shape
+    HL = w_query.shape[1] // HEAD_DIM
+    HZ = HL // NZ
+    W = HZ * HEAD_DIM
+    HEADS = HL * NY
+    SLOTS = cache_keys.shape[1]
+    DO = w_out.shape[1]
+    CH = 512
+    NCH = DO // CH
+    half = HEAD_DIM // 2
+    KV = w_keyval.shape[1]
+    angles = rotary_angles(positions, HEAD_DIM)
+    bf16, f32 = jnp.bfloat16, jnp.float32
+    V = pltpu.VMEM
+    D = pltpu.SemaphoreType.DMA
+    slots_q = min(HL, 8)
+    peers = NZ * NY - 1
+    anyspec = pl.BlockSpec(memory_space=pl.ANY)
+    vspec = pl.BlockSpec(memory_space=pltpu.VMEM)
+    scratch = [
+        V((slots_q, DZ, HEAD_DIM), bf16), V((DZ, KV), bf16), V((NCH, w_out.shape[0], CH), bf16),
+        V((R, SLOTS, HEAD_DIM), bf16), V((R, SLOTS + 16, HEAD_DIM), bf16),
+        V((R * NY, DZ), bf16), V((HL, R * NY, HEAD_DIM), f32), V((HL - HZ, R * NY, HEAD_DIM), f32),
+        V((R * NY, KV), f32), V((NZ - 1, R * NY, KV), f32), V((R * NY, KV), bf16), V((NY, R, KV), bf16),
+        V((R * NY, W), bf16), V((R, HEADS * HEAD_DIM), bf16),
+        V((HEADS * R, half), f32), V((HEADS * R, half), f32), V((R, 2 * HEAD_DIM), f32),
+        V((R, SLOTS, HEADS), f32), V((R, HEADS), f32),
+        V((2, R, 128), f32), V((NZ - 1, 2, R, 128), f32), V((R, 128), f32), V((R, 128), f32),
+        V((HEADS * R, half), f32), V((HEADS * R, half), f32),
+        V((NZ - 1, HL * R, half), f32), V((NZ - 1, HL * R, half), f32),
+        V((R * NY, W), bf16), V((R * NY, HL * HEAD_DIM), bf16),
+        V((NCH, R * NY, CH), f32), V((NY - 1, NCH, R, CH), f32),
+        D((slots_q,)), D((4,)), D((NCH,)), D((NY - 1,)), D((NY - 1,)),
+        D((HL - HZ,)), D((HL - HZ,)), D, D((NZ - 1,)), D((NY - 1,)), D((NY - 1,)),
+        D((peers,)), D((peers,)), D((NZ - 1,)), D((NZ - 1,)),
+        D((NZ - 1,)), D((NZ - 1,)), D((NZ - 1,)), D((NZ - 1,)),
+        D((peers,)), D((peers,)), D((NY - 1, NCH)), D((NY - 1, NCH)),
+    ]
+    return pl.pallas_call(
+        functools.partial(fused_kernel, (NZ, NY, R, HL, SLOTS, CH, NCH)),
+        out_shape=jax.ShapeDtypeStruct((R, DO), bf16),
+        in_specs=[pl.BlockSpec(memory_space=pltpu.SMEM), anyspec, vspec, vspec] + [anyspec] * 5,
+        out_specs=vspec,
+        scratch_shapes=scratch,
+        compiler_params=pltpu.CompilerParams(
+            collective_id=0, has_side_effects=True, vmem_limit_bytes=VMEM_LIMIT
+        ),
+    )(lengths, tokens, jnp.cos(angles), jnp.sin(angles), w_query, w_keyval, w_out, cache_keys, cache_values)
+
+
 def solution(mesh):
     placed = (
         P(("ga", "yz"), "gx"),
@@ -134,6 +545,13 @@
         P(("ga", "yz")),
         P(("ga", "yz")),
     )
-    return jax.shard_map(
-        body, mesh=mesh, in_specs=placed, out_specs=P(("ga", "yz"), "gx"), check_vma=False
-    )
+
+    def run(*arrays):
+        chosen = body
+        if fits(mesh, arrays[1]):
+            chosen = functools.partial(fused_body, mesh.shape["gx"], mesh.shape["yz"])
+        return jax.shard_map(
+            chosen, mesh=mesh, in_specs=placed, out_specs=P(("ga", "yz"), "gx"), check_vma=False
+        )(*arrays)
+
+    return run

time: 212 us -> 105 us (0.50)
  Pallas kernels: 0 us -> 102 us
  blocking collectives: 83.6 us -> 0 us
  waiting for transfers between devices: 68.6 us -> 0 us
  matrix products: 29.5 us -> 0 us
  between operations: 13.6 us -> 0.01 us
  starting transfers between devices: 6.8 us -> 0 us
  other arithmetic: 7.26 us -> 1.39 us
    pallas_call x0 -> x1, Pallas kernels: none -> 102 us  [fused_body(): pl.pallas_call(functools.partial(fused_kernel, (NZ, NY, R, HL, SLOTS, CH,...]
    psum x1 -> x0, blocking collectives: 37.8 us -> none  [body(): query_sum, keyval_sum = lax.psum((query_part, keyval_part), 'gx')]
    all_gather x3 -> x0, blocking collectives: 35.9 us -> none  [the longest x2 26.6 us: merged(): everything = jax.tree.map(lambda part: lax.all_gather(part, axis), array)]
    all_gather x1 -> x0, waiting for transfers between devices: 34 us -> none  [merged(): everything = jax.tree.map(lambda part: lax.all_gather(part, axis), array)]
    dot_general x6 -> x0, matrix products: 29.5 us -> none  [the longest x1 12.6 us: body(): jnp.dot(block_rows, w_out, preferred_element_type=jnp.float32)]
    reduce_scatter x1 -> x0, waiting for transfers between devices: 23.7 us -> none  [body(): lax.psum_scatter(jnp.dot(block_rows, w_out, preferred_element_type=jnp.fl...]
    all_to_all x2 -> x0, waiting for transfers between devices: 10.9 us -> none  [the longest x1 7.21 us: body(): lax.all_to_all(query_full, 'yz', split_axis=0, concat_axis=1, tiled=True)]
    all_to_all x1 -> x0, blocking collectives: 9.89 us -> none  [body(): lax.all_to_all(out_heads, 'yz', split_axis=1, concat_axis=0, tiled=True)]
  transfers between devices with their start and end apart: 4 -> 0, of which waited for: 4 -> 0; matrix products, arithmetic and copies ran while one was open for 1% -> 0% of each run, Pallas kernels for 0% -> 0%
where the time goes in v1:
time: 105 us
  Pallas kernels  102 us (97%)
  local copies, waits for them, and re-layouts  1.58 us (2%)
  other arithmetic  1.39 us (1%)
    pallas_call x1, Pallas kernels, fused_body(): pl.pallas_call(functools.partial(fused_kernel, (NZ, NY, R, HL, SLOTS, CH,...  102 us

profile of v1, /device:TPU:0, one launch (start us, length us, event | category | flops | bytes accessed | tf_op | source)
XLA Modules:
  0.0 104.6 jit_solution(13209809485554068004)
XLA Ops:
  0.0 0.7 convert_element_type.3
  0.7 0.7 multiply_sine_fusion
  1.4 101.6 %shard_map.82 = bf16[16,4608]{1,0:T(8,128)(2,1)} custom-call(s32[16]{0:T(128)} %len_ref.1, bf16[16,4608]{1,0:T(8,128)(2,1)} %tok_ref.1, f32[16,128]{1,0:T(8,128)} %get-tuple-element.6.cos_ref, f32[16,128]{1,0:T(8,128)} %get-tuple-element.5.sin_ref, bf16[4608,3072]{1,0:T(8,128)(2,1)} %wq_ref.1, bf16[4608,128]{1,0:T(8,128)(2,1)} %wkv_ref.1, ...), custom_call_target="tpu_custom_call" | custom-call | tf_op jit(solution)/shard_map/pallas_call | solution.py:525
  103.0 1.6 %copy.10 = bf16[16,4608]{1,0:T(8,128)(2,1)} copy(bf16[16,4608]{1,0:T(8,128)(2,1)} %shard_map.82) | data formatting | bytes 294912
  (1 shorter events, 0.0 us)

commit v2 on v1

--- a/solution.py
+++ b/solution.py
@@ -131,7 +131,7 @@
 def fits(mesh, w_query):
     z_count, y_count = mesh.shape["gx"], mesh.shape["yz"]
     heads_local = w_query.shape[1] // HEAD_DIM // y_count
-    return heads_local % z_count == 0 and z_count > 1 and y_count > 1 and (w_query.shape[0] // z_count) % 512 == 0
+    return z_count == 4 and y_count == 4 and heads_local % 4 == 0
 
 
 def split3(x):
@@ -170,7 +170,7 @@
     SLOTSQ = wq.shape[0]
 
     def wq_copy(n):
-        owner = lax.rem(z + n // HZ + 1, NZ)
+        owner = z ^ (NZ - 1 - n // HZ)
         col = pl.multiple_of((owner * HZ + n % HZ) * HEAD_DIM, HEAD_DIM)
         slot = lax.rem(n, SLOTSQ)
         return pltpu.make_async_copy(wq_ref.at[:, pl.ds(col, HEAD_DIM)], wq.at[slot], wq_sem.at[slot])
@@ -190,11 +190,15 @@
 
     pl.semaphore_wait(barrier, NZ * NY - 1)
 
-    def tok_copy(d):
-        return remote(tok_ref, tok.at[own_rows, :], tok_s.at[d - 1], tok_r.at[d - 1], peer(0, d))
-
-    for d in range(1, NY):
-        tok_copy(d).start()
+    far_rows = pl.ds(pl.multiple_of((y ^ 2) * R, R), R)
+
+    def tok_copy(k):
+        src = tok.at[far_rows, :] if k == 2 else tok_ref
+        rows = far_rows if k == 2 else own_rows
+        return remote(src, tok.at[rows, :], tok_s.at[k], tok_r.at[k], {"gx": z, "yz": y ^ (2 if k == 1 else 1)})
+
+    tok_copy(1).start()
+    tok_copy(0).start()
     wkv_local.start()
 
     @pl.loop(0, SLOTSQ)
@@ -208,9 +212,11 @@
         col = pl.multiple_of(n * CH, CH)
         return pltpu.make_async_copy(wo_ref.at[:, pl.ds(col, CH)], wo.at[n], wo_sem.at[n])
 
+    tok_copy(1).wait_recv()
+    tok_copy(2).start()
     tok_local.wait()
-    for d in range(1, NY):
-        tok_copy(d).wait_recv()
+    tok_copy(0).wait_recv()
+    tok_copy(2).wait_recv()
 
     wkv_local.wait()
     kvp[...] = jnp.dot(tok[...], wkv[...], preferred_element_type=f32)
@@ -223,8 +229,8 @@
         def _():
             kv_copy(src - 1).start()
 
-    def rs_copy(n):
-        return remote(part.at[n], rbuf.at[n], rs_s.at[n], rs_r.at[n], peer(n // HZ + 1, 0))
+    def rs_copy(n, step):
+        return remote(part.at[n], rbuf.at[n], rs_s.at[n], rs_r.at[n], {"gx": z ^ (2 if step == 1 else 1), "yz": y})
 
     def project(n):
         wq_copy(n).wait()
@@ -236,10 +242,22 @@
 
     REM = HL - HZ
 
-    @pl.loop(0, REM)
+    @pl.loop(0, HZ)
     def _(n):
         project(n)
-        rs_copy(n).start()
+        rs_copy(n, 0).start()
+
+    @pl.loop(HZ, 2 * HZ)
+    def _(n):
+        project(n)
+        rs_copy(n - HZ, 0).wait_recv()
+        part[n] = part[n] + rbuf[n - HZ]
+        rs_copy(n, 1).start()
+
+    @pl.loop(2 * HZ, REM)
+    def _(n):
+        project(n)
+        rs_copy(n, 2).start()
 
     @pl.loop(REM, HL)
     def _(n):
@@ -271,9 +289,9 @@
 
     for i in range(HZ):
         total = part[REM + i]
-        for d in range(1, NZ):
-            n = (d - 1) * HZ + i
-            rs_copy(n).wait_recv()
+        for step in (2, 1):
+            n = step * HZ + i
+            rs_copy(n, step).wait_recv()
             total = total + rbuf[n]
         qs[:, i * HEAD_DIM:(i + 1) * HEAD_DIM] = total.astype(jnp.bfloat16)
 
@@ -425,34 +443,52 @@
 
     xin[own_rows, z_cols] = hs[own_rows, :]
 
-    @pl.loop(1, NZ * NY)
-    def _(o):
-        hd_copy(o).wait_recv()
-
-    def po_copy(n, d):
-        target = lax.rem(y + d, NY)
+    def po_copy(n, k):
+        target = y ^ (1, 3, 2)[k]
         rows = pl.ds(pl.multiple_of(target * R, R), R)
         return remote(
-            pout.at[n, rows, :], prc.at[d - 1, n], po_s.at[d - 1, n], po_r.at[d - 1, n], peer(0, d)
+            pout.at[n, rows, :], prc.at[k, n], po_s.at[k, n], po_r.at[k, n], {"gx": z, "yz": y ^ (1, 1, 2)[k]}
         )
 
+    def cross(n):
+        po_copy(n, 1).wait_recv()
+        pout[n, far_rows, :] = pout[n, far_rows, :] + prc[1, n]
+        po_copy(n, 2).start()
+
+    for dz in range(NZ):
+        @pl.loop(max(1, dz * NY), (dz + 1) * NY)
+        def _(o):
+            hd_copy(o).wait_recv()
+
+        depth = pl.ds(pl.multiple_of(lax.rem(z + NZ - dz, NZ) * W, W), W)
+        block = xin[:, depth]
+
+        @pl.loop(0, NCH)
+        def _(n):
+            if dz == 0:
+                wo_copy(n).wait()
+            product = jnp.dot(block, wo[n, depth, :], preferred_element_type=f32)
+            pout[n] = product if dz == 0 else pout[n] + product
+            if dz == NZ - 1:
+                po_copy(n, 1).start()
+                po_copy(n, 0).start()
+
+                @pl.when(n > 0)
+                def _():
+                    cross(n - 1)
+
+    cross(NCH - 1)
+
     @pl.loop(0, NCH)
     def _(n):
-        wo_copy(n).wait()
-        pout[n] = jnp.dot(xin[...], wo[n], preferred_element_type=f32)
-        for d in range(1, NY):
-            po_copy(n, d).start()
-
-    @pl.loop(0, NCH)
-    def _(n):
         total = pout[n, own_rows, :]
-        for d in range(1, NY):
-            po_copy(n, d).wait_recv()
-            total = total + prc[d - 1, n]
+        for k in (0, 2):
+            po_copy(n, k).wait_recv()
+            total = total + prc[k, n]
         out_ref[:, pl.ds(pl.multiple_of(n * CH, CH), CH)] = total.astype(jnp.bfloat16)
 
-    for d in range(1, NY):
-        tok_copy(d).wait_send()
+    for k in range(3):
+        tok_copy(k).wait_send()
     for src in range(1, NZ):
         @pl.when(z == src)
         def _():
@@ -463,9 +499,10 @@
         for d in range(1, NY):
             kv2_copy(d).wait_send()
 
-    @pl.loop(0, REM)
-    def _(n):
-        rs_copy(n).wait_send()
+    for step in range(3):
+        @pl.loop(step * HZ, (step + 1) * HZ)
+        def _(n):
+            rs_copy(n, step).wait_send()
 
     @pl.loop(1, NZ * NY)
     def _(o):
@@ -479,8 +516,8 @@
 
     @pl.loop(0, NCH)
     def _(n):
-        for d in range(1, NY):
-            po_copy(n, d).wait_send()
+        for k in range(3):
+            po_copy(n, k).wait_send()
 
 
 def fused_body(NZ, NY, tokens, w_query, w_keyval, w_out, cache_keys, cache_values, lengths, positions):

time: 105 us -> 102 us (0.971)
  Pallas kernels: 102 us -> 98.8 us
    pallas_call x1, Pallas kernels: 102 us -> 98.8 us  [fused_body(): pl.pallas_call(functools.partial(fused_kernel, (NZ, NY, R, HL, SLOTS, CH,...]
where the time goes in v2:
time: 102 us
  Pallas kernels  98.8 us (97%)
  local copies, waits for them, and re-layouts  1.58 us (2%)
  other arithmetic  1.39 us (1%)
    pallas_call x1, Pallas kernels, fused_body(): pl.pallas_call(functools.partial(fused_kernel, (NZ, NY, R, HL, SLOTS, CH,...  98.8 us

profile of v2, /device:TPU:0, one launch (start us, length us, event | category | flops | bytes accessed | tf_op | source)
XLA Modules:
  0.0 101.8 jit_solution(13346300743656719167)
XLA Ops:
  0.0 0.7 convert_element_type.3
  0.7 0.7 multiply_sine_fusion
  1.4 98.8 %shard_map.82 = bf16[16,4608]{1,0:T(8,128)(2,1)} custom-call(s32[16]{0:T(128)} %len_ref.1, bf16[16,4608]{1,0:T(8,128)(2,1)} %tok_ref.1, f32[16,128]{1,0:T(8,128)} %get-tuple-element.6.cos_ref, f32[16,128]{1,0:T(8,128)} %get-tuple-element.5.sin_ref, bf16[4608,3072]{1,0:T(8,128)(2,1)} %wq_ref.1, bf16[4608,128]{1,0:T(8,128)(2,1)} %wkv_ref.1, ...), custom_call_target="tpu_custom_call" | custom-call | tf_op jit(solution)/shard_map/pallas_call | solution.py:562
  100.2 1.6 %copy.10 = bf16[16,4608]{1,0:T(8,128)(2,1)} copy(bf16[16,4608]{1,0:T(8,128)(2,1)} %shard_map.82) | data formatting | bytes 294912
  (1 shorter events, 0.0 us)

commit v3 on v1

--- a/solution.py
+++ b/solution.py
@@ -131,7 +131,7 @@
 def fits(mesh, w_query):
     z_count, y_count = mesh.shape["gx"], mesh.shape["yz"]
     heads_local = w_query.shape[1] // HEAD_DIM // y_count
-    return heads_local % z_count == 0 and z_count > 1 and y_count > 1 and (w_query.shape[0] // z_count) % 512 == 0
+    return z_count == 4 and y_count == 4 and heads_local % 4 == 0
 
 
 def split3(x):
@@ -147,7 +147,7 @@
     len_ref, tok_ref, cos_ref, sin_ref, wq_ref, wkv_ref, wo_ref, ck_ref, cv_ref,
     out_ref,
     wq, wkv, wo, kc, vc, tok, part, rbuf, kvp, kvr, kvs, kvin, qs, qin, ra, rb, rk,
-    s_buf, sn_buf, st, str_, mg, lg, oa, ob, oar, obr, hs, xin, pout, prc,
+    st, str_, oa, ob, oar, obr, hs, xin, pout, prc,
     wq_sem, misc_sem, wo_sem, tok_s, tok_r, rs_s, rs_r, kv_s, kv_r, kv2_s, kv2_r,
     qd_s, qd_r, st_s, st_r, oa_s, oa_r, ob_s, ob_r, hd_s, hd_r, po_s, po_r,
 ):
@@ -180,7 +180,7 @@
     tok_local.start()
     wkv_local = pltpu.make_async_copy(wkv_ref, wkv, misc_sem.at[1])
     kc_local = pltpu.make_async_copy(ck_ref, kc, misc_sem.at[2])
-    vc_local = pltpu.make_async_copy(cv_ref, vc.at[:, pl.ds(0, SLOTS), :], misc_sem.at[3])
+    vc_local = pltpu.make_async_copy(cv_ref, vc, misc_sem.at[3])
 
     barrier = pltpu.get_barrier_semaphore()
 
@@ -189,6 +189,8 @@
         pl.semaphore_signal(barrier, inc=1, device_id=peer(o // NY, o % NY), device_id_type=MESH)
 
     pl.semaphore_wait(barrier, NZ * NY - 1)
+
+    far_rows = pl.ds(pl.multiple_of((y ^ 2) * R, R), R)
 
     def tok_copy(d):
         return remote(tok_ref, tok.at[own_rows, :], tok_s.at[d - 1], tok_r.at[d - 1], peer(0, d))
@@ -331,8 +333,18 @@
     over_first = (((0,), (0,)), ((), ()))
     first_z = z == 0
 
-    @pl.loop(0, R)
-    def _(r):
+    HALF = R // 2
+
+    def o_copies(part_rows, d):
+        target = lax.rem(z + d, NZ)
+        size = HL * HALF
+        rows = pl.ds(pl.multiple_of((part_rows * NZ + target) * size, size), size)
+        return tuple(
+            remote(src.at[rows, :], dst.at[d - 1, part_rows], snd.at[d - 1, part_rows], rcv.at[d - 1, part_rows], peer(d, 0))
+            for src, dst, snd, rcv in ((oa, oar, oa_s, oa_r), (ob, obr, ob_s, ob_r))
+        )
+
+    def attend(r):
         picked = pl.ds(r, HEADS, stride=R)
         q = jnp.concatenate([ra[picked, :], rb[picked, :]], axis=1)
         keys = kc[r]
@@ -346,15 +358,27 @@
         )[0:1, :] * scale
         s_new = jnp.where(first_z, s_new, f32(-1e30))
         peak = jnp.maximum(jnp.max(s, axis=0, keepdims=True), s_new)
-        mass = jnp.sum(jnp.where(visible, jnp.exp(s - peak), f32(0.0)), axis=0, keepdims=True)
-        mass = mass + jnp.where(first_z, jnp.exp(s_new - peak), f32(0.0))
-        s_buf[r] = s
-        sn_buf[pl.ds(r, 1), :] = s_new
+        p = jnp.where(visible, jnp.exp(s - peak), f32(0.0))
+        p_new = jnp.where(first_z, jnp.exp(s_new - peak), f32(0.0))
         st[0, pl.ds(r, 1), 0:HEADS] = peak
-        st[1, pl.ds(r, 1), 0:HEADS] = mass
+        st[1, pl.ds(r, 1), 0:HEADS] = jnp.sum(p, axis=0, keepdims=True) + p_new
         row = lax.broadcasted_iota(jnp.int32, (16, HEAD_DIM), 0)
         value = jnp.broadcast_to(rk[pl.ds(r, 1), HEAD_DIM:], (16, HEAD_DIM))
-        vc[r, SLOTS:SLOTS + 16, :] = jnp.where(row == 0, value, f32(0.0)).astype(jnp.bfloat16)
+        value = jnp.where(row == 0, value, f32(0.0)).astype(jnp.bfloat16)
+        values = jnp.concatenate([vc[r, 0:SLOTS, :], value], axis=0)
+        row = lax.broadcasted_iota(jnp.int32, (16, HEADS), 0)
+        p_new = jnp.where(row == 0, jnp.broadcast_to(p_new, (16, HEADS)), f32(0.0))
+        p_all = jnp.concatenate([p, p_new], axis=0)
+        acc = sum(lax.dot_general(piece, values, over_first, preferred_element_type=f32) for piece in split3(p_all))
+        placed = pl.ds(r // HALF * (HEADS * HALF) + r % HALF, HEADS, stride=HALF)
+        oa[placed, :] = acc[:, :half]
+        ob[placed, :] = acc[:, half:]
+
+    for part_rows in range(2):
+        pl.loop(part_rows * HALF, (part_rows + 1) * HALF)(attend)
+        for d in range(1, NZ):
+            for copy in o_copies(part_rows, d):
+                copy.start()
 
     def st_copy(d):
         return remote(st, str_.at[d - 1], st_s.at[d - 1], st_r.at[d - 1], peer(d, 0))
@@ -363,54 +387,32 @@
         st_copy(d).start()
     for d in range(1, NZ):
         st_copy(d).wait_recv()
-    peak = st[0]
-    for d in range(1, NZ):
-        peak = jnp.maximum(peak, str_[d - 1, 0])
-    mass = st[1] * jnp.exp(st[0] - peak)
-    for d in range(1, NZ):
-        mass = mass + str_[d - 1, 1] * jnp.exp(str_[d - 1, 0] - peak)
-    mg[...] = peak
-    lg[...] = mass
-
-    @pl.loop(0, R)
-    def _(r):
-        peak = mg[pl.ds(r, 1), 0:HEADS]
-        mass = lg[pl.ds(r, 1), 0:HEADS]
-        p = jnp.exp(s_buf[r] - peak) / mass
-        p_new = jnp.exp(sn_buf[pl.ds(r, 1), :] - peak) / mass
-        row = lax.broadcasted_iota(jnp.int32, (16, HEADS), 0)
-        p_new = jnp.where(row == 0, jnp.broadcast_to(p_new, (16, HEADS)), f32(0.0))
-        p_all = jnp.concatenate([p, p_new], axis=0)
-        values = vc[r]
-        acc = sum(lax.dot_general(piece, values, over_first, preferred_element_type=f32) for piece in split3(p_all))
-        picked = pl.ds(r, HEADS, stride=R)
-        oa[picked, :] = acc[:, :half]
-        ob[picked, :] = acc[:, half:]
-
-    def o_copies(d):
-        target = lax.rem(z + d, NZ)
-        rows = pl.ds(pl.multiple_of(target * HL * R, HL * R), HL * R)
-        return (
-            remote(oa.at[rows, :], oar.at[d - 1], oa_s.at[d - 1], oa_r.at[d - 1], peer(d, 0)),
-            remote(ob.at[rows, :], obr.at[d - 1], ob_s.at[d - 1], ob_r.at[d - 1], peer(d, 0)),
-        )
-
-    for d in range(1, NZ):
-        for copy in o_copies(d):
-            copy.start()
-    for d in range(1, NZ):
-        for copy in o_copies(d):
-            copy.wait_recv()
+    peaks = [st[0]] + [str_[d - 1, 0] for d in range(1, NZ)]
+    masses = [st[1]] + [str_[d - 1, 1] for d in range(1, NZ)]
+    highest = functools.reduce(jnp.maximum, peaks)
+    factors = [jnp.exp(peak - highest) for peak in peaks]
+    normaliser = sum(mass * factor for mass, factor in zip(masses, factors))
+    factors = [factor / normaliser for factor in factors]
+    lane = lax.broadcasted_iota(jnp.int32, (R, 128), 1)
+    for part_rows in range(2):
+        for d in range(1, NZ):
+            for copy in o_copies(part_rows, d):
+                copy.wait_recv()
     for k in range(HL):
-        rows = pl.ds(pl.multiple_of(z * HL * R + k * R, R), R)
-        ta = oa[rows, :]
-        tb = ob[rows, :]
-        for d in range(1, NZ):
-            ta = ta + oar[d - 1, k * R:(k + 1) * R, :]
-            tb = tb + obr[d - 1, k * R:(k + 1) * R, :]
+        columns = [
+            jnp.sum(jnp.where(lane == z * HL + k, factor, f32(0.0)), axis=1, keepdims=True) for factor in factors
+        ]
         block, i = k // HZ, k % HZ
-        hs[block * R:(block + 1) * R, i * HEAD_DIM:i * HEAD_DIM + half] = ta.astype(jnp.bfloat16)
-        hs[block * R:(block + 1) * R, i * HEAD_DIM + half:(i + 1) * HEAD_DIM] = tb.astype(jnp.bfloat16)
+        for own, arrived, low in ((oa, oar, 0), (ob, obr, half)):
+            pieces = []
+            for h in range(2):
+                mine = own[pl.ds(pl.multiple_of((h * NZ + z) * HL * HALF + k * HALF, HALF), HALF), :]
+                total = mine * columns[0][h * HALF:(h + 1) * HALF]
+                for d in range(1, NZ):
+                    total = total + arrived[d - 1, h, k * HALF:(k + 1) * HALF, :] * columns[d][h * HALF:(h + 1) * HALF]
+                pieces.append(total)
+            both = jnp.concatenate(pieces, axis=0).astype(jnp.bfloat16)
+            hs[block * R:(block + 1) * R, i * HEAD_DIM + low:i * HEAD_DIM + low + half] = both
 
     z_cols = pl.ds(pl.multiple_of(z * W, W), W)
 
@@ -425,30 +427,48 @@
 
     xin[own_rows, z_cols] = hs[own_rows, :]
 
-    @pl.loop(1, NZ * NY)
-    def _(o):
-        hd_copy(o).wait_recv()
-
-    def po_copy(n, d):
-        target = lax.rem(y + d, NY)
+    def po_copy(n, k):
+        target = y ^ (1, 3, 2)[k]
         rows = pl.ds(pl.multiple_of(target * R, R), R)
         return remote(
-            pout.at[n, rows, :], prc.at[d - 1, n], po_s.at[d - 1, n], po_r.at[d - 1, n], peer(0, d)
+            pout.at[n, rows, :], prc.at[k, n], po_s.at[k, n], po_r.at[k, n], {"gx": z, "yz": y ^ (1, 1, 2)[k]}
         )
 
+    def cross(n):
+        po_copy(n, 1).wait_recv()
+        pout[n, far_rows, :] = pout[n, far_rows, :] + prc[1, n]
+        po_copy(n, 2).start()
+
+    for dz in range(NZ):
+        @pl.loop(max(1, dz * NY), (dz + 1) * NY)
+        def _(o):
+            hd_copy(o).wait_recv()
+
+        depth = pl.ds(pl.multiple_of(lax.rem(z + NZ - dz, NZ) * W, W), W)
+        block = xin[:, depth]
+
+        @pl.loop(0, NCH)
+        def _(n):
+            if dz == 0:
+                wo_copy(n).wait()
+            product = jnp.dot(block, wo[n, depth, :], preferred_element_type=f32)
+            pout[n] = product if dz == 0 else pout[n] + product
+            if dz == NZ - 1:
+                po_copy(n, 1).start()
+                po_copy(n, 0).start()
+
+                @pl.when(n > 0)
+                def _():
+                    cross(n - 1)
+
+    cross(NCH - 1)
+
     @pl.loop(0, NCH)
     def _(n):
-        wo_copy(n).wait()
-        pout[n] = jnp.dot(xin[...], wo[n], preferred_element_type=f32)
-        for d in range(1, NY):
-            po_copy(n, d).start()
-
-    @pl.loop(0, NCH)
-    def _(n):
         total = pout[n, own_rows, :]
-        for d in range(1, NY):
-            po_copy(n, d).wait_recv()
-            total = total + prc[d - 1, n]
+        for k in (0, 2):
+            po_copy(n, k).wait_recv()
+            total = total + prc[k, n]
         out_ref[:, pl.ds(pl.multiple_of(n * CH, CH), CH)] = total.astype(jnp.bfloat16)
 
     for d in range(1, NY):
@@ -474,13 +494,14 @@
 
     for d in range(1, NZ):
         st_copy(d).wait_send()
-        for copy in o_copies(d):
-            copy.wait_send()
+        for part_rows in range(2):
+            for copy in o_copies(part_rows, d):
+                copy.wait_send()
 
     @pl.loop(0, NCH)
     def _(n):
-        for d in range(1, NY):
-            po_copy(n, d).wait_send()
+        for k in range(3):
+            po_copy(n, k).wait_send()
 
 
 def fused_body(NZ, NY, tokens, w_query, w_keyval, w_out, cache_keys, cache_values, lengths, positions):
@@ -505,21 +526,20 @@
     vspec = pl.BlockSpec(memory_space=pltpu.VMEM)
     scratch = [
         V((slots_q, DZ, HEAD_DIM), bf16), V((DZ, KV), bf16), V((NCH, w_out.shape[0], CH), bf16),
-        V((R, SLOTS, HEAD_DIM), bf16), V((R, SLOTS + 16, HEAD_DIM), bf16),
+        V((R, SLOTS, HEAD_DIM), bf16), V((R, SLOTS, HEAD_DIM), bf16),
         V((R * NY, DZ), bf16), V((HL, R * NY, HEAD_DIM), f32), V((HL - HZ, R * NY, HEAD_DIM), f32),
         V((R * NY, KV), f32), V((NZ - 1, R * NY, KV), f32), V((R * NY, KV), bf16), V((NY, R, KV), bf16),
         V((R * NY, W), bf16), V((R, HEADS * HEAD_DIM), bf16),
         V((HEADS * R, half), f32), V((HEADS * R, half), f32), V((R, 2 * HEAD_DIM), f32),
-        V((R, SLOTS, HEADS), f32), V((R, HEADS), f32),
-        V((2, R, 128), f32), V((NZ - 1, 2, R, 128), f32), V((R, 128), f32), V((R, 128), f32),
+        V((2, R, 128), f32), V((NZ - 1, 2, R, 128), f32),
         V((HEADS * R, half), f32), V((HEADS * R, half), f32),
-        V((NZ - 1, HL * R, half), f32), V((NZ - 1, HL * R, half), f32),
+        V((NZ - 1, 2, HL * R // 2, half), f32), V((NZ - 1, 2, HL * R // 2, half), f32),
         V((R * NY, W), bf16), V((R * NY, HL * HEAD_DIM), bf16),
         V((NCH, R * NY, CH), f32), V((NY - 1, NCH, R, CH), f32),
         D((slots_q,)), D((4,)), D((NCH,)), D((NY - 1,)), D((NY - 1,)),
         D((HL - HZ,)), D((HL - HZ,)), D, D((NZ - 1,)), D((NY - 1,)), D((NY - 1,)),
         D((peers,)), D((peers,)), D((NZ - 1,)), D((NZ - 1,)),
-        D((NZ - 1,)), D((NZ - 1,)), D((NZ - 1,)), D((NZ - 1,)),
+        D((NZ - 1, 2)), D((NZ - 1, 2)), D((NZ - 1, 2)), D((NZ - 1, 2)),
         D((peers,)), D((peers,)), D((NY - 1, NCH)), D((NY - 1, NCH)),
     ]
     return pl.pallas_call(

time: 105 us -> 94.2 us (0.90)
  Pallas kernels: 102 us -> 91 us
    pallas_call x1, Pallas kernels: 102 us -> 91 us  [fused_body(): pl.pallas_call(functools.partial(fused_kernel, (NZ, NY, R, HL, SLOTS, CH,...]
where the time goes in v3:
time: 94.2 us; the launch traced here: 94 us
  Pallas kernels  91 us (97%)
  local copies, waits for them, and re-layouts  1.58 us (2%)
  other arithmetic  1.39 us (1%)
    pallas_call x1, Pallas kernels, fused_body(): pl.pallas_call(functools.partial(fused_kernel, (NZ, NY, R, HL, SLOTS, CH,...  91 us

profile of v3, /device:TPU:0, one launch (start us, length us, event | category | flops | bytes accessed | tf_op | source)
XLA Modules:
  0.0 94.0 jit_solution(16654689154705699617)
XLA Ops:
  0.0 0.7 convert_element_type.3
  0.7 0.7 multiply_sine_fusion
  1.4 91.0 %shard_map.82 = bf16[16,4608]{1,0:T(8,128)(2,1)} custom-call(s32[16]{0:T(128)} %len_ref.1, bf16[16,4608]{1,0:T(8,128)(2,1)} %tok_ref.1, f32[16,128]{1,0:T(8,128)} %get-tuple-element.6.cos_ref, f32[16,128]{1,0:T(8,128)} %get-tuple-element.5.sin_ref, bf16[4608,3072]{1,0:T(8,128)(2,1)} %wq_ref.1, bf16[4608,128]{1,0:T(8,128)(2,1)} %wkv_ref.1, ...), custom_call_target="tpu_custom_call" | custom-call | tf_op jit(solution)/shard_map/pallas_call | solution.py:545
  92.4 1.6 %copy.10 = bf16[16,4608]{1,0:T(8,128)(2,1)} copy(bf16[16,4608]{1,0:T(8,128)(2,1)} %shard_map.82) | data formatting | bytes 294912
  (1 shorter events, 0.0 us)
